TPU v7x, 32 devices: a whole 2x2x4 slice. The times are simulated.
32 devices in a mesh: dp: 16 (over z, y, x), tensor: 2 (over core).
Axes of the slice: x: 2, y: 2, z: 4, core: 2. Of those that a mesh axis runs over, the one named last changes fastest.
Arguments:
- activations: bfloat16 [20480, 5120], P('dp', 'tensor'), may hold values from -6 to 6
- cotangents: bfloat16 [20480, 1024], P('dp', 'tensor'), as said below
- error_old: bfloat16 [81920, 1024], P(('dp', 'tensor')), may hold values from -3 to 3
- pause_positions: int32 [320], replicated, may hold values from 0 to 1279, as said below
- initial_q: float32 [1024, 32], replicated, may hold values from -6 to 6
Outputs:
- error_new: bfloat16 [81920, 1024], P(('dp', 'tensor'))
- q_factor: float32 [1024, 32], P('tensor')
Inputs may be any that keep to these rules, and one draw needn't show every extreme that they name: pause_positions holds 320 different padding positions of a replica's batch, which attention masks out, in no particular order; they are the same for every replica. cotangents lie within 6 / sqrt(1280) in magnitude.
All inputs are finite; a program needn't handle non-finite values.
Results may differ from a plain program's by a relative error of at most 0.002.
Values may be sent and summed in bfloat16 or wider, within the bound.
A program may use at most 64 MiB of HBM per device.

v0:
```python
import jax
import jax.numpy as jnp
from jax import lax
from jax.sharding import PartitionSpec as P


def kept_mask(pause_positions, row_count):
    positions = jnp.arange(row_count, dtype=jnp.int32)
    struck = jnp.any(positions[:, None] == pause_positions[None, :], axis=1)
    return jnp.where(struck, 0, 1).astype(jnp.int32)


def cholesky_pass(matrix):
    contract = (((0,), (0,)), ((), ()))
    gram = lax.dot_general(matrix, matrix, contract, precision=lax.Precision.HIGHEST)
    factor_low = jnp.linalg.cholesky(gram)
    return lax.linalg.triangular_solve(
        factor_low, matrix, left_side=False, lower=True, transpose_a=True
    )


def body(activations, cotangents, error_old, pause_positions, initial_q):
    row_count = activations.shape[0]
    contract = (((0,), (0,)), ((), ()))
    kept = kept_mask(pause_positions, row_count)
    cot_rows = cotangents * kept.astype(jnp.bfloat16)[:, None]
    gradient = lax.dot_general(
        activations,
        lax.all_gather(cot_rows, "tensor", axis=1, tiled=True),
        contract,
        preferred_element_type=jnp.float32,
    )
    merged = gradient + error_old.astype(jnp.float32)
    replicas = lax.axis_size("dp")
    local_left = jnp.dot(merged, initial_q, precision=lax.Precision.HIGHEST)
    left_raw = lax.psum(local_left, "dp") / replicas
    own_rows = left_raw.shape[0]
    gathered = lax.all_gather(left_raw, "tensor", axis=0, tiled=True)
    whole_basis = cholesky_pass(cholesky_pass(gathered))
    left_basis = lax.dynamic_slice_in_dim(
        whole_basis, lax.axis_index("tensor") * own_rows, own_rows, 0
    )
    partial_q = lax.dot_general(merged, left_basis, contract, precision=lax.Precision.HIGHEST)
    own_q = lax.psum_scatter(
        partial_q.astype(jnp.bfloat16), "tensor", scatter_dimension=0, tiled=True
    ).astype(jnp.float32)
    own_q = lax.psum(own_q, "dp") / replicas
    q_full = lax.all_gather(own_q, "tensor", axis=0, tiled=True)
    update = jnp.dot(left_basis, q_full.T, precision=lax.Precision.HIGHEST)
    return ((merged - update).astype(jnp.bfloat16), own_q)


def solution(mesh):
    return jax.shard_map(
        body,
        mesh=mesh,
        in_specs=(P("dp", "tensor"), P("dp", "tensor"), P(("dp", "tensor"), None), P(), P()),
        out_specs=(P(("dp", "tensor"), None), P("tensor", None)),
        check_vma=False,
    )
```

profile of v0, /device:TPU:0, one launch (start us, length us, event | category | flops | bytes accessed | tf_op | source)
XLA Modules:
  0.0 302.6 jit_solution(2455262347405460462)
XLA Ops:
  7.2 1.0 fusion
  8.2 2.6 broadcast_multiply_fusion
  11.0 7.9 %copy.12 = bf16[2560,1024]{0,1:T(8,128)(2,1)} copy(bf16[2560,1024]{1,0:T(8,128)(2,1)} %param.10) | data formatting | bytes 10485760 | tf_op args[2]
  18.9 6.2 %all-gather.2.cloned.1.call-done = bf16[1280,1024]{1,0:T(8,128)(2,1)} async-done(((bf16[1280,512]{1,0:T(8,128)(2,1)}), bf16[1280,1024]{1,0:T(8,128)(2,1)}) %all-gather.2.cloned.1.call-update) | async-done | bytes 2621456 | tf_op jit(solution)/shard_map/all_gather | solution.py:29
  25.1 11.1 %bitcast_add_fusion = f32[2560,1024]{0,1:T(8,128)S(1)} fusion(bf16[2560,1024]{0,1:T(8,128)(2,1)} %copy.12, bf16[1280,1024]{1,0:T(8,128)(2,1)} %all-gather.2.cloned.1.call-done, bf16[1280,2560]{1,0:T(8,128)(2,1)} %param.8), kind=kOutput, calls=%fused_computation | convolution fusion | flops 6716129280 | bytes 24903680 | tf_op jit(solution)/shard_map/dot_general | solution.py:27
  36.3 4.0 %copy-done.1 = f32[2560,1024]{0,1:T(8,128)} copy-done((f32[2560,1024]{0,1:T(8,128)}, f32[2560,1024]{0,1:T(8,128)S(1)}, u32[]{:S(2)}) %copy-start.1) | copy-done | bytes 10485784
  40.3 7.1 %fusion.13 = f32[2560,32]{0,1:T(8,128)} fusion(f32[2560,1024]{0,1:T(8,128)S(1)} %bitcast_add_fusion, f32[1024,32]{0,1:T(8,128)S(1)} %copy-done), kind=kOutput, calls=%fused_computation.32 | convolution fusion | flops 1006632960 | bytes 10944512 | tf_op jit(solution)/shard_map/dot_general | solution.py:35
  47.5 108.8 %all-reduce.3.cloned.1.call-done = f32[2560,32]{0,1:T(8,128)} async-done(((f32[2560,32]{0,1:T(8,128)}), f32[2560,32]{0,1:T(8,128)}) %all-reduce.3.cloned.1.call-update) | async-done | bytes 327696 | tf_op jit(solution)/shard_map/psum | solution.py:36
  156.3 1.0 broadcast_multiply_fusion.1
  157.3 2.5 all_gather.10
  159.7 0.7 fusion.14
  160.5 2.9 cholesky.44
  164.7 2.4 custom-call.6
  167.2 0.8 convolution_bitcast_fusion.1
  167.9 0.7 fusion.15
  168.7 2.9 cholesky.55
  172.9 2.4 custom-call.7
  175.4 0.8 convolution_bitcast_fusion
  176.1 12.8 %convolution_convert_fusion = bf16[1024,32]{0,1:T(8,128)(2,1)} fusion(f32[2560,1024]{0,1:T(8,128)} %copy-done.1, f32[5120,32]{0,1:T(8,128)S(1)} %convolution_bitcast_fusion, s32[]{:T(128)S(6)} %select_n.15), kind=kOutput, calls=%fused_computation.6 | convolution fusion | flops 1006665728 | bytes 10878980 | tf_op jit(solution)/shard_map/dot_general | solution.py:43
  188.9 6.6 %reduce-scatter.2.cloned.1.call-done = bf16[512,32]{0,1:T(8,128)(2,1)} async-done(((bf16[1024,32]{0,1:T(8,128)(2,1)}), bf16[512,32]{0,1:T(8,128)(2,1)}) %reduce-scatter.2.cloned.1.call-update) | async-done | bytes 32784 | tf_op jit(solution)/shard_map/reduce_scatter | solution.py:44
  195.6 77.7 %all-reduce.4 = f32[512,32]{0,1:T(8,128)S(1)} all-reduce(bf16[512,32]{0,1:T(8,128)(2,1)} %reduce-scatter.2.cloned.1.call-done), channel_id=1, replica_groups=mesh['dp'=16,'tensor'=2] {'dp'}, use_global_device_ids=true, to_apply=%region_5.8 | all-reduce | flops 16384 | bytes 98304 | tf_op jit(solution)/shard_map/psum | solution.py:47
  273.3 2.1 all_gather.11
  275.4 12.7 %subtract_convert_fusion = bf16[2560,1024]{0,1:T(8,128)(2,1)} fusion(f32[2560,1024]{0,1:T(8,128)} %copy-done.1, f32[1024,32]{0,1:T(8,128)S(1)} %all_gather.11, f32[5120,32]{0,1:T(8,128)S(1)} %convolution_bitcast_fusion, s32[]{:T(128)S(6)} %select_n.15), kind=kOutput, calls=%fused_computation.1 | convolution fusion | flops 1011875840 | bytes 16187396 | tf_op jit(solution)/shard_map/dot_general | solution.py:49
  288.1 7.9 %copy.16 = bf16[2560,1024]{1,0:T(8,128)(2,1)} copy(bf16[2560,1024]{0,1:T(8,128)(2,1)} %subtract_convert_fusion) | data formatting | bytes 10485760
  (23 shorter events, 3.0 us)
Async XLA Ops:
  7.2 33.1 %copy-start = (f32[1024,32]{0,1:T(8,128)S(1)}, f32[1024,32]{0,1:T(8,128)}, u32[]{:S(2)}) copy-start(f32[1024,32]{0,1:T(8,128)} %param.12) | copy-start | bytes 393220
  7.2 17.9 %all-gather.2.cloned.1.call-start = ((), (), s32[]{:S(2)}) async-start(), calls=%async_computation.1 | async-start | bytes 3932160 | tf_op jit(solution)/shard_map/all_gather | solution.py:29
  10.9 145.4 %all-reduce.3.cloned.1.call-start = ((), (), s32[]{:S(2)}) async-start(), calls=%async_computation.2 | async-start | bytes 655360 | tf_op jit(solution)/shard_map/psum | solution.py:36
  36.3 4.0 %copy-start.1 = (f32[2560,1024]{0,1:T(8,128)}, f32[2560,1024]{0,1:T(8,128)S(1)}, u32[]{:S(2)}) copy-start(f32[2560,1024]{0,1:T(8,128)S(1)} %bitcast_add_fusion) | copy-start | bytes 31457284
  47.4 148.2 %reduce-scatter.2.cloned.1.call-start = ((), (), s32[]{:S(2)}) async-start(), calls=%async_computation.3 | async-start | bytes 98304 | tf_op jit(solution)/shard_map/reduce_scatter | solution.py:44
  273.3 14.8 %copy-start.2 = (f32[512,32]{0,1:T(8,128)}, f32[512,32]{0,1:T(8,128)S(1)}, u32[]{:S(2)}) copy-start(f32[512,32]{0,1:T(8,128)S(1)} %broadcast_multiply_fusion.2) | copy-start | bytes 196612
Sparse Core Ops, SparseCore 0:
  11.0 14.0 all-gather.1
  47.5 108.7 all-reduce.2
  189.1 6.4 reduce-scatter.1
where the time goes:
time: 303 us
  waiting for transfers between devices  122 us (40%)
  blocking collectives  82.3 us (27%)
  matrix products  46.6 us (15%)
  local copies, waits for them, and re-layouts  20 us (7%)
  other arithmetic  18 us (6%)
  between operations  13.9 us (5%)
    psum x1, waiting for transfers between devices, body(): left_raw = lax.psum(local_left, 'dp') / replicas  109 us
    psum x1, blocking collectives, body(): own_q = lax.psum(own_q, 'dp') / replicas  77.7 us
    unnamed x8, local copies, waits for them, and re-layouts  19.8 us
    dot_general x1, matrix products, body(): lax.dot_general(merged, left_basis, contract, precision=lax.Precision.HIG...  12.8 us
    dot_general x1, matrix products, body(): update = jnp.dot(left_basis, q_full.T, precision=lax.Precision.HIGHEST)  12.7 us
    dot_general x1, matrix products, body(): lax.dot_general(activations, lax.all_gather(cot_rows, 'tensor', axis=1, t...  11.1 us
    another operation x6, other arithmetic, cholesky_pass(): factor_low = jnp.linalg.cholesky(gram)  7.19 us
    dot_general x1, matrix products, body(): local_left = jnp.dot(merged, initial_q, precision=lax.Precision.HIGHEST)  7.13 us
  transfers between devices with their start and end apart: 3, of which 3 were waited for; matrix products, arithmetic and copies ran while one was open for 3% of the time, Pallas kernels for 0%

commit v1 on v0

v1 whole, which is shorter than its diff:
```python
import functools
import math

import jax
import jax.numpy as jnp
from jax import lax
from jax.experimental import pallas as pl
from jax.experimental.pallas import tpu as pltpu
from jax.sharding import PartitionSpec as P

F32 = jnp.float32
BF16 = jnp.bfloat16
NN = (((1,), (0,)), ((), ()))
NT = (((1,), (1,)), ((), ()))
TN = (((0,), (0,)), ((), ()))


def mm(a, b, dims):
    return lax.dot_general(a, b, dims, preferred_element_type=F32)


def mm_high(a, b, dims):
    return lax.dot_general(
        a, b, dims, preferred_element_type=F32, precision=lax.Precision.HIGHEST
    )


def pieces(x):
    high = x.astype(BF16)
    rest = x - high.astype(F32)
    middle = rest.astype(BF16)
    low = (rest - middle.astype(F32)).astype(BF16)
    return high, middle, low


def stacked(x):
    return jnp.concatenate(pieces(x), axis=0)


def folded(x):
    n = x.shape[0] // 3
    return x[:n] + x[n : 2 * n] + x[2 * n :]


def inverse_cholesky(gram):
    n = gram.shape[0]
    rows = lax.broadcasted_iota(jnp.int32, (n, n), 0)
    cols = lax.broadcasted_iota(jnp.int32, (n, n), 1)
    left = gram
    right = jnp.where(rows == cols, 1.0, 0.0).astype(F32)
    pivots = jnp.ones((n, n), F32)
    for k in range(n):
        pivot = left[k : k + 1, k : k + 1]
        column = jnp.broadcast_to(left[:, k : k + 1], (n, n))
        pivots = jnp.where(rows == k, jnp.broadcast_to(pivot, (n, n)), pivots)
        factor = jnp.where(rows > k, column / pivot, 0.0)
        left = left - factor * left[k : k + 1, :]
        right = right - factor * right[k : k + 1, :]
    return right / jnp.sqrt(pivots)


def kernel(
    sizes, act_hbm, cot_hbm, err_hbm, pause_ref, q0_ref, out_hbm, q_ref,
    act, cot, err, merged, left_all, left3, parts, sums, sum_in, qall, pcat,
    xa1, ra1, xb1, rb1, gd1, xa2, ra2, xb2, rb2, gd2,
    load_sem, out_sem, t_send, t_recv, s1, r1, s2, r2,
):
    replicas, outer, inner, tens = sizes
    d = lax.axis_index("dp")
    t = lax.axis_index("tensor")
    o, i = d // inner, lax.rem(d, inner)
    row_count, width = act.shape
    kt = cot.shape[2]
    rank = q0_ref.shape[1]

    load_err = pltpu.make_async_copy(err_hbm, err, load_sem.at[0])
    load_cot = pltpu.make_async_copy(cot_hbm, cot.at[t], load_sem.at[1])
    load_act = pltpu.make_async_copy(act_hbm, act, load_sem.at[2])
    load_err.start()
    load_cot.start()
    load_act.start()

    def outer_peer(k):
        return (lax.rem(o + k, outer) * inner + i, t)

    def inner_peer(k):
        return (o * inner + lax.rem(i + k, inner), t)

    def tensor_peer(k):
        return (d, lax.rem(t + k, tens))

    barrier = pltpu.get_barrier_semaphore()
    peers = [outer_peer(k) for k in range(1, outer)]
    peers += [inner_peer(k) for k in range(1, inner)]
    peers += [tensor_peer(k) for k in range(1, tens)]
    for peer in peers:
        pl.semaphore_signal(barrier, inc=1, device_id=peer, device_id_type=pl.DeviceIdType.MESH)
    pl.semaphore_wait(barrier, len(peers))

    sent = []

    def send(src, dst, send_sem, recv_sem, peer):
        copy = pltpu.make_async_remote_copy(
            src_ref=src, dst_ref=dst, send_sem=send_sem, recv_sem=recv_sem,
            device_id=peer, device_id_type=pl.DeviceIdType.MESH,
        )
        copy.start()
        sent.append(copy)
        return copy

    cot_copies = [
        send(cot_hbm, cot.at[t], t_send.at[0, k], t_recv.at[0, k], tensor_peer(k))
        for k in range(1, tens)
    ]

    positions = lax.broadcasted_iota(jnp.int32, (row_count, pause_ref.shape[1]), 0)
    hits = jnp.sum(jnp.where(positions == pause_ref[...], 1.0, 0.0), axis=1, keepdims=True)
    kept = jnp.where(hits == 0.0, 1.0, 0.0).astype(BF16)
    q3 = stacked(q0_ref[...].T)

    load_err.wait()
    from_err = mm(q3, err[...], NT)
    load_cot.wait()
    for copy in cot_copies:
        copy.wait_recv()
    for s in range(tens):
        cot[s] = cot[s] * kept
    tok = mm(q3[:, :kt], cot[0], NT)
    for s in range(1, tens):
        tok = tok + mm(q3[:, s * kt : (s + 1) * kt], cot[s], NT)
    tok3 = stacked(folded(tok))
    load_act.wait()
    own_left = folded(mm(tok3, act[...], NN) + from_err) * (1.0 / replicas)

    tile = math.gcd(width, 256)

    def gradient_tiles(first, last):
        @pl.loop(first, last)
        def _(j):
            here = pl.ds(pl.multiple_of(j * tile, tile), tile)
            block = act[:, here]
            for s in range(tens):
                outs = slice(s * kt, (s + 1) * kt)
                merged[here, outs] = mm(block, cot[s], TN) + err[here, outs].astype(F32)

    def all_reduce(value, bufs, ss, rs, work):
        xa, ra, xb, rb, gd = bufs
        h, span = xa.shape[1], value.shape[1]
        cw = xb.shape[2]
        if span < xa.shape[2]:
            xa[...] = jnp.zeros(xa.shape, F32)
        for p in range(inner):
            xa[p, :, :span] = value[p * h : (p + 1) * h]
        copies = [
            send(xa.at[lax.rem(i + k, inner)], ra.at[k], ss.at[0, k], rs.at[0, k], inner_peer(k))
            for k in range(1, inner)
        ]
        work[0]()
        total = xa[i]
        for k, copy in enumerate(copies, 1):
            copy.wait_recv()
            total = total + ra[k]
        for p in range(outer):
            xb[p] = total[:, p * cw : (p + 1) * cw]
        copies = [
            send(xb.at[lax.rem(o + k, outer)], rb.at[k], ss.at[1, k], rs.at[1, k], outer_peer(k))
            for k in range(1, outer)
        ]
        work[1]()
        total = xb[o]
        for k, copy in enumerate(copies, 1):
            copy.wait_recv()
            total = total + rb[k]
        gd[i, o] = total
        copies = [
            send(gd.at[i, o], gd.at[i, o], ss.at[2, k], rs.at[2, k], outer_peer(k))
            for k in range(1, outer)
        ]
        work[2]()
        for copy in copies:
            copy.wait_recv()
        copies = [
            send(gd.at[i], gd.at[i], ss.at[3, k], rs.at[3, k], inner_peer(k))
            for k in range(1, inner)
        ]
        work[3]()
        for copy in copies:
            copy.wait_recv()
        bands = [
            jnp.concatenate([gd[p, c] for c in range(outer)], axis=1)[:, :span]
            for p in range(inner)
        ]
        return jnp.concatenate(bands, axis=0)

    tiles = width // tile
    marks = [tiles * n // 10 for n in (0, 4, 6, 7, 10)]
    left = all_reduce(
        own_left, (xa1, ra1, xb1, rb1, gd1), s1, r1,
        [functools.partial(gradient_tiles, marks[n], marks[n + 1]) for n in range(4)],
    )
    left_all[t] = left
    left_copies = [
        send(left_all.at[t], left_all.at[t], t_send.at[1, k], t_recv.at[1, k], tensor_peer(k))
        for k in range(1, tens)
    ]

    left3[...] = stacked(left)
    v3 = stacked(folded(mm(left3[...], act[...], NT)))
    s_err = mm(left3[...], err[...], NN)
    for s in range(tens):
        total = s_err[:, s * kt : (s + 1) * kt] + mm(v3, cot[s], NN)
        parts[s] = folded(total) * (1.0 / replicas)
    copies = [
        send(parts.at[lax.rem(t + k, tens)], sum_in.at[k], t_send.at[2, k], t_recv.at[2, k], tensor_peer(k))
        for k in range(1, tens)
    ]

    def first_pass():
        for copy in left_copies:
            copy.wait_recv()
        gram = mm_high(left_all[0], left_all[0], NT)
        for s in range(1, tens):
            gram = gram + mm_high(left_all[s], left_all[s], NT)
        return inverse_cholesky(gram)

    inv1 = first_pass()
    total = parts[t]
    for k, copy in enumerate(copies, 1):
        copy.wait_recv()
        total = total + sum_in[k]

    held = {}

    def second_pass():
        own = mm_high(inv1, left_all[t], NN)
        gram = jnp.zeros((rank, rank), F32)
        for s in range(tens):
            basis = mm_high(inv1, left_all[s], NN)
            gram = gram + mm_high(basis, basis, NT)
        held["inv2"] = inverse_cholesky(gram)
        held["own"] = own

    def own_basis():
        high, middle, _ = pieces(mm_high(held["inv2"], held["own"], NN))
        pcat[...] = jnp.concatenate([high, middle, high], axis=0)

    def nothing():
        pass

    total = all_reduce(
        total, (xa2, ra2, xb2, rb2, gd2), s2, r2, [second_pass, own_basis, nothing, nothing]
    )
    own_q = mm_high(held["inv2"], mm_high(inv1, total, NN), NN)
    qall[t] = own_q
    copies = [
        send(qall.at[t], qall.at[t], t_send.at[3, k], t_recv.at[3, k], tensor_peer(k))
        for k in range(1, tens)
    ]
    q_ref[...] = own_q.T
    for copy in copies:
        copy.wait_recv()

    qcats = []
    for s in range(tens):
        high, middle, _ = pieces(qall[s])
        qcats.append(jnp.concatenate([high, high, middle], axis=0))

    for j in range(tiles):
        here = slice(j * tile, (j + 1) * tile)
        for s in range(tens):
            outs = slice(s * kt, (s + 1) * kt)
            update = mm(pcat[:, here], qcats[s], TN)
            err[here, outs] = (merged[here, outs] - update).astype(BF16)
        pltpu.make_async_copy(err.at[here], out_hbm.at[here], out_sem.at[j]).start()
    for j in range(tiles):
        here = slice(j * tile, (j + 1) * tile)
        pltpu.make_async_copy(err.at[here], out_hbm.at[here], out_sem.at[j]).wait()
    for copy in sent:
        copy.wait_send()


def solution(mesh):
    replicas, tens = mesh.shape["dp"], mesh.shape["tensor"]
    inner = 1
    while inner * inner < replicas or replicas % inner:
        inner += 1
    outer = replicas // inner

    def body(activations, cotangents, error_old, pause_positions, initial_q):
        rows, width = activations.shape
        kt = cotangents.shape[1]
        kw, rank = initial_q.shape
        h = rank // inner
        tile = math.gcd(width, 256)

        def reduce_bufs(span):
            cw = -(-span // (128 * outer)) * 128
            return [
                pltpu.VMEM((inner, h, cw * outer), F32),
                pltpu.VMEM((inner, h, cw * outer), F32),
                pltpu.VMEM((outer, h, cw), F32),
                pltpu.VMEM((outer, h, cw), F32),
                pltpu.VMEM((inner, outer, h, cw), F32),
            ]

        most = max(inner, outer)
        anywhere = pl.BlockSpec(memory_space=pl.ANY)
        vmem = pl.BlockSpec(memory_space=pltpu.VMEM)
        dma = pltpu.SemaphoreType.DMA
        error_new, q = pl.pallas_call(
            functools.partial(kernel, (replicas, outer, inner, tens)),
            out_shape=(
                jax.ShapeDtypeStruct(error_old.shape, BF16),
                jax.ShapeDtypeStruct((kt, rank), F32),
            ),
            in_specs=[anywhere, anywhere, anywhere, vmem, vmem],
            out_specs=(anywhere, vmem),
            scratch_shapes=[
                pltpu.VMEM((rows, width), BF16),
                pltpu.VMEM((tens, rows, kt), BF16),
                pltpu.VMEM((width, kw), BF16),
                pltpu.VMEM((width, kw), F32),
                pltpu.VMEM((tens, rank, width), F32),
                pltpu.VMEM((3 * rank, width), BF16),
                pltpu.VMEM((tens, rank, kt), F32),
                pltpu.VMEM((tens, rank, kt), F32),
                pltpu.VMEM((tens, rank, kt), F32),
                pltpu.VMEM((tens, rank, kt), F32),
                pltpu.VMEM((3 * rank, width), BF16),
                *reduce_bufs(width),
                *reduce_bufs(kt),
                dma((3,)),
                dma((width // tile,)),
                dma((4, tens)),
                dma((4, tens)),
                dma((4, most)),
                dma((4, most)),
                dma((4, most)),
                dma((4, most)),
            ],
            compiler_params=pltpu.CompilerParams(
                collective_id=0, has_side_effects=True, vmem_limit_bytes=56 * 1024 * 1024
            ),
            cost_estimate=pl.CostEstimate(
                flops=2 * rows * width * kw, bytes_accessed=2 * rows * width + 4 * width * kw, transcendentals=0
            ),
        )(activations, cotangents, error_old, pause_positions.reshape(1, -1), initial_q)
        return error_new, q

    return jax.shard_map(
        body,
        mesh=mesh,
        in_specs=(P("dp", "tensor"), P("dp", "tensor"), P(("dp", "tensor"), None), P(), P()),
        out_specs=(P(("dp", "tensor"), None), P("tensor", None)),
        check_vma=False,
    )
```

time: 303 us -> 71.9 us (0.24)
  waiting for transfers between devices: 122 us -> 0 us
  blocking collectives: 82.3 us -> 0 us
  Pallas kernels: 0 us -> 60.1 us
  matrix products: 46.6 us -> 0 us
  other arithmetic: 18 us -> 0 us
  between operations: 13.9 us -> 0.64 us
  local copies, waits for them, and re-layouts: 20 us -> 10.3 us
    psum x1 -> x0, waiting for transfers between devices: 109 us -> none  [body(): left_raw = lax.psum(local_left, 'dp') / replicas]
    psum x1 -> x0, blocking collectives: 77.7 us -> none  [body(): own_q = lax.psum(own_q, 'dp') / replicas]
    pallas_call x0 -> x1, Pallas kernels: none -> 60.1 us  [body(): pl.pallas_call(functools.partial(kernel, (replicas, outer, inner, tens)),...]
    dot_general x6 -> x0, matrix products: 45.1 us -> none  [the longest x1 12.8 us: body(): lax.dot_general(merged, left_basis, contract, precision=lax.Precision.HIG...]
    another operation x10 -> x0, other arithmetic: 13.4 us -> none  [the longest x6 7.19 us: cholesky_pass(): factor_low = jnp.linalg.cholesky(gram)]
    unnamed x8 -> x2, local copies, waits for them, and re-layouts: 19.8 us -> 7.32 us
    reduce_scatter x1 -> x0, waiting for transfers between devices: 6.64 us -> none  [body(): lax.psum_scatter(partial_q.astype(jnp.bfloat16), 'tensor', scatter_dimens...]
    all_gather x1 -> x0, waiting for transfers between devices: 6.24 us -> none  [body(): lax.all_gather(cot_rows, 'tensor', axis=1, tiled=True)]
  transfers between devices with their start and end apart: 3 -> 0, of which waited for: 3 -> 0; matrix products, arithmetic and copies ran while one was open for 3% -> 0% of each run, Pallas kernels for 0% -> 0%
where the time goes in v1:
time: 71.9 us; the launch traced here: 71 us
  Pallas kernels  60.1 us (84%)
  local copies, waits for them, and re-layouts  10.3 us (14%)
    pallas_call x1, Pallas kernels, body(): pl.pallas_call(functools.partial(kernel, (replicas, outer, inner, tens)),...  60.1 us
    unnamed x2, local copies, waits for them, and re-layouts  7.32 us
    pallas_call x1, local copies, waits for them, and re-layouts, body(): pl.pallas_call(functools.partial(kernel, (replicas, outer, inner, tens)),...  1.69 us

profile of v1, /device:TPU:0, one launch (start us, length us, event | category | flops | bytes accessed | tf_op | source)
XLA Modules:
  0.0 71.0 jit_solution(7817271287121609609)
XLA Ops:
  0.6 1.2 %reshape.7.pause_ref = s32[1,320]{1,0:T(1,128)} reshape(s32[320]{0:T(512)} %param.8) | data formatting | bytes 2560 | tf_op jit(solution)/shard_map/reshape | solution.py:347
  1.9 1.9 %copy.7.q0_ref = f32[1024,32]{1,0:T(8,128)} copy(f32[1024,32]{0,1:T(8,128)} %param.9) | data formatting | bytes 262144 | tf_op args[4]
  3.8 60.1 %shard_map.68 = (bf16[2560,1024]{1,0:T(8,128)(2,1)}, f32[512,32]{1,0:T(8,128)}) custom-call(bf16[1280,2560]{1,0:T(8,128)(2,1)} %act_hbm.1, bf16[1280,512]{1,0:T(8,128)(2,1)} %cot_hbm.1, bf16[2560,1024]{1,0:T(8,128)(2,1)} %err_hbm.1, s32[1,320]{1,0:T(1,128)} %reshape.7.pause_ref, f32[1024,32]{1,0:T(8,128)} %copy.7.q0_ref), custom_call_target="tpu_custom_call" | custom-call | flops 6710886400 | bytes 17039360 | tf_op jit(solution)/shard_map/pallas_call | solution.py:310
  63.9 1.7 %copy.8 = f32[512,32]{0,1:T(8,128)} copy(f32[512,32]{1,0:T(8,128)} %get-tuple-element.3) | data formatting | bytes 131072 | tf_op jit(solution)/shard_map/pallas_call | solution.py:310
  65.6 5.4 %copy.10 = bf16[2560,1024]{1,0:T(8,128)(2,1)} copy(bf16[2560,1024]{1,0:T(8,128)(2,1)} %get-tuple-element.6) | data formatting | bytes 10485760

commit v2 on v1

--- a/solution.py
+++ b/solution.py
@@ -40,6 +40,16 @@
 def folded(x):
     n = x.shape[0] // 3
     return x[:n] + x[n : 2 * n] + x[2 * n :]
+
+
+def gram_of(x3):
+    g = folded(mm(x3, x3, NT))
+    n = g.shape[0]
+    return g[:, :n] + g[:, n : 2 * n] + g[:, 2 * n :]
+
+
+def applied(matrix, x3):
+    return folded(mm(stacked(jnp.concatenate([matrix] * 3, axis=1)), x3, NN))
 
 
 def inverse_cholesky(gram):
@@ -50,20 +60,22 @@
     right = jnp.where(rows == cols, 1.0, 0.0).astype(F32)
     pivots = jnp.ones((n, n), F32)
     for k in range(n):
-        pivot = left[k : k + 1, k : k + 1]
         column = jnp.broadcast_to(left[:, k : k + 1], (n, n))
-        pivots = jnp.where(rows == k, jnp.broadcast_to(pivot, (n, n)), pivots)
-        factor = jnp.where(rows > k, column / pivot, 0.0)
-        left = left - factor * left[k : k + 1, :]
-        right = right - factor * right[k : k + 1, :]
+        pivots = jnp.where(rows == k, column, pivots)
+        scale = 1.0 / column[k : k + 1, :]
+        column = jnp.where(rows > k, column, 0.0)
+        left_row = left[k : k + 1, :] * scale
+        right_row = right[k : k + 1, :] * scale
+        left = left - column * left_row
+        right = right - column * right_row
     return right / jnp.sqrt(pivots)
 
 
 def kernel(
-    sizes, act_hbm, cot_hbm, err_hbm, pause_ref, q0_ref, out_hbm, q_ref,
-    act, cot, err, merged, left_all, left3, parts, sums, sum_in, qall, pcat,
+    sizes, act_hbm, cot_hbm, err_hbm, pause_ref, q0_ref, merged, pcat, qcat, q_ref,
+    act, cot, err, left_all, left3, parts, sum_in, qall,
     xa1, ra1, xb1, rb1, gd1, xa2, ra2, xb2, rb2, gd2,
-    load_sem, out_sem, t_send, t_recv, s1, r1, s2, r2,
+    load_sem, t_send, t_recv, s1, r1, s2, r2,
 ):
     replicas, outer, inner, tens = sizes
     d = lax.axis_index("dp")
@@ -71,7 +83,7 @@
     o, i = d // inner, lax.rem(d, inner)
     row_count, width = act.shape
     kt = cot.shape[2]
-    rank = q0_ref.shape[1]
+    rank = q0_ref.shape[0]
 
     load_err = pltpu.make_async_copy(err_hbm, err, load_sem.at[0])
     load_cot = pltpu.make_async_copy(cot_hbm, cot.at[t], load_sem.at[1])
@@ -113,10 +125,10 @@
         for k in range(1, tens)
     ]
 
-    positions = lax.broadcasted_iota(jnp.int32, (row_count, pause_ref.shape[1]), 0)
-    hits = jnp.sum(jnp.where(positions == pause_ref[...], 1.0, 0.0), axis=1, keepdims=True)
+    positions = lax.broadcasted_iota(jnp.int32, (row_count, pause_ref.shape[0]), 0)
+    hits = jnp.sum(jnp.where(positions == pause_ref[...].reshape(1, -1), 1.0, 0.0), axis=1, keepdims=True)
     kept = jnp.where(hits == 0.0, 1.0, 0.0).astype(BF16)
-    q3 = stacked(q0_ref[...].T)
+    q3 = stacked(q0_ref[...])
 
     load_err.wait()
     from_err = mm(q3, err[...], NT)
@@ -193,7 +205,7 @@
         return jnp.concatenate(bands, axis=0)
 
     tiles = width // tile
-    marks = [tiles * n // 10 for n in (0, 4, 6, 7, 10)]
+    marks = [tiles * n // 10 for n in (0, 3, 5, 7, 10)]
     left = all_reduce(
         own_left, (xa1, ra1, xb1, rb1, gd1), s1, r1,
         [functools.partial(gradient_tiles, marks[n], marks[n + 1]) for n in range(4)],
@@ -204,9 +216,19 @@
         for k in range(1, tens)
     ]
 
-    left3[...] = stacked(left)
-    v3 = stacked(folded(mm(left3[...], act[...], NT)))
-    s_err = mm(left3[...], err[...], NN)
+    own3 = stacked(left)
+    left3[t] = own3
+    v3 = stacked(folded(mm(own3, act[...], NT)))
+    for copy in left_copies:
+        copy.wait_recv()
+    for k in range(1, tens):
+        peer = lax.rem(t + k, tens)
+        left3[peer] = stacked(left_all[peer])
+    gram = gram_of(left3[0])
+    for s in range(1, tens):
+        gram = gram + gram_of(left3[s])
+    inv1 = inverse_cholesky(gram)
+    s_err = mm(left3[t], err[...], NN)
     for s in range(tens):
         total = s_err[:, s * kt : (s + 1) * kt] + mm(v3, cot[s], NN)
         parts[s] = folded(total) * (1.0 / replicas)
@@ -214,69 +236,66 @@
         send(parts.at[lax.rem(t + k, tens)], sum_in.at[k], t_send.at[2, k], t_recv.at[2, k], tensor_peer(k))
         for k in range(1, tens)
     ]
-
-    def first_pass():
-        for copy in left_copies:
-            copy.wait_recv()
-        gram = mm_high(left_all[0], left_all[0], NT)
-        for s in range(1, tens):
-            gram = gram + mm_high(left_all[s], left_all[s], NT)
-        return inverse_cholesky(gram)
-
-    inv1 = first_pass()
+    held = {}
+
+    def second_gram():
+        gram = jnp.zeros((rank, rank), F32)
+        for s in range(tens):
+            basis3 = stacked(applied(inv1, left3[s]))
+            left3[s] = basis3
+            gram = gram + gram_of(basis3)
+        held["gram"] = gram
+
+    def second_inverse():
+        held["inv2"] = inverse_cholesky(held["gram"])
+        held["both"] = mm_high(held["inv2"], inv1, NN)
+
+    def own_basis():
+        high, middle, _ = pieces(applied(held["inv2"], left3[t]))
+        pcat[...] = jnp.concatenate([high, middle, high], axis=0)
+
+    def nothing():
+        pass
+
+    second_gram()
     total = parts[t]
     for k, copy in enumerate(copies, 1):
         copy.wait_recv()
         total = total + sum_in[k]
-
-    held = {}
-
-    def second_pass():
-        own = mm_high(inv1, left_all[t], NN)
-        gram = jnp.zeros((rank, rank), F32)
-        for s in range(tens):
-            basis = mm_high(inv1, left_all[s], NN)
-            gram = gram + mm_high(basis, basis, NT)
-        held["inv2"] = inverse_cholesky(gram)
-        held["own"] = own
-
-    def own_basis():
-        high, middle, _ = pieces(mm_high(held["inv2"], held["own"], NN))
-        pcat[...] = jnp.concatenate([high, middle, high], axis=0)
-
-    def nothing():
-        pass
-
     total = all_reduce(
-        total, (xa2, ra2, xb2, rb2, gd2), s2, r2, [second_pass, own_basis, nothing, nothing]
+        total, (xa2, ra2, xb2, rb2, gd2), s2, r2, [second_inverse, own_basis, nothing, nothing]
     )
-    own_q = mm_high(held["inv2"], mm_high(inv1, total, NN), NN)
+    own_q = mm_high(held["both"], total, NN)
     qall[t] = own_q
     copies = [
         send(qall.at[t], qall.at[t], t_send.at[3, k], t_recv.at[3, k], tensor_peer(k))
         for k in range(1, tens)
     ]
-    q_ref[...] = own_q.T
+    q_ref[...] = own_q
     for copy in copies:
         copy.wait_recv()
-
-    qcats = []
     for s in range(tens):
         high, middle, _ = pieces(qall[s])
-        qcats.append(jnp.concatenate([high, high, middle], axis=0))
-
-    for j in range(tiles):
+        qcat[s] = jnp.concatenate([high, high, middle], axis=0)
+    for copy in sent:
+        copy.wait_send()
+
+
+def update_kernel(tile, merged, pcat, qcat, q_in, out_hbm, q_out, out, sems):
+    tens, _, kt = qcat.shape
+    copies = []
+    for j in range(out.shape[0] // tile):
         here = slice(j * tile, (j + 1) * tile)
         for s in range(tens):
             outs = slice(s * kt, (s + 1) * kt)
-            update = mm(pcat[:, here], qcats[s], TN)
-            err[here, outs] = (merged[here, outs] - update).astype(BF16)
-        pltpu.make_async_copy(err.at[here], out_hbm.at[here], out_sem.at[j]).start()
-    for j in range(tiles):
-        here = slice(j * tile, (j + 1) * tile)
-        pltpu.make_async_copy(err.at[here], out_hbm.at[here], out_sem.at[j]).wait()
-    for copy in sent:
-        copy.wait_send()
+            update = mm(pcat[:, here], qcat[s], TN)
+            out[here, outs] = (merged[here, outs] - update).astype(BF16)
+        copy = pltpu.make_async_copy(out.at[here], out_hbm.at[here], sems.at[j])
+        copy.start()
+        copies.append(copy)
+    q_out[...] = q_in[...]
+    for copy in copies:
+        copy.wait()
 
 
 def solution(mesh):
@@ -290,6 +309,7 @@
         rows, width = activations.shape
         kt = cotangents.shape[1]
         kw, rank = initial_q.shape
+        mib = 1024 * 1024
         h = rank // inner
         tile = math.gcd(width, 256)
 
@@ -304,33 +324,31 @@
             ]
 
         most = max(inner, outer)
-        anywhere = pl.BlockSpec(memory_space=pl.ANY)
+        hbm = pl.BlockSpec(memory_space=pltpu.HBM)
         vmem = pl.BlockSpec(memory_space=pltpu.VMEM)
         dma = pltpu.SemaphoreType.DMA
-        error_new, q = pl.pallas_call(
+        merged, pcat, qcat, own_q = pl.pallas_call(
             functools.partial(kernel, (replicas, outer, inner, tens)),
             out_shape=(
-                jax.ShapeDtypeStruct(error_old.shape, BF16),
-                jax.ShapeDtypeStruct((kt, rank), F32),
+                pltpu.VMEM((width, kw), F32),
+                pltpu.VMEM((3 * rank, width), BF16),
+                pltpu.VMEM((tens, 3 * rank, kt), BF16),
+                pltpu.VMEM((rank, kt), F32),
             ),
-            in_specs=[anywhere, anywhere, anywhere, vmem, vmem],
-            out_specs=(anywhere, vmem),
+            in_specs=[hbm, hbm, hbm, vmem, vmem],
+            out_specs=(vmem,) * 4,
             scratch_shapes=[
                 pltpu.VMEM((rows, width), BF16),
                 pltpu.VMEM((tens, rows, kt), BF16),
                 pltpu.VMEM((width, kw), BF16),
-                pltpu.VMEM((width, kw), F32),
                 pltpu.VMEM((tens, rank, width), F32),
-                pltpu.VMEM((3 * rank, width), BF16),
+                pltpu.VMEM((tens, 3 * rank, width), BF16),
                 pltpu.VMEM((tens, rank, kt), F32),
                 pltpu.VMEM((tens, rank, kt), F32),
                 pltpu.VMEM((tens, rank, kt), F32),
-                pltpu.VMEM((tens, rank, kt), F32),
-                pltpu.VMEM((3 * rank, width), BF16),
                 *reduce_bufs(width),
                 *reduce_bufs(kt),
                 dma((3,)),
-                dma((width // tile,)),
                 dma((4, tens)),
                 dma((4, tens)),
                 dma((4, most)),
@@ -339,13 +357,27 @@
                 dma((4, most)),
             ],
             compiler_params=pltpu.CompilerParams(
-                collective_id=0, has_side_effects=True, vmem_limit_bytes=56 * 1024 * 1024
+                collective_id=0, has_side_effects=True, vmem_limit_bytes=36 * mib
             ),
             cost_estimate=pl.CostEstimate(
                 flops=2 * rows * width * kw, bytes_accessed=2 * rows * width + 4 * width * kw, transcendentals=0
             ),
-        )(activations, cotangents, error_old, pause_positions.reshape(1, -1), initial_q)
-        return error_new, q
+        )(*(
+            pltpu.with_memory_space_constraint(x, pltpu.HBM)
+            for x in (activations, cotangents, error_old, pause_positions, initial_q.T)
+        ))
+        error_new, q = pl.pallas_call(
+            functools.partial(update_kernel, tile),
+            out_shape=(
+                jax.ShapeDtypeStruct(error_old.shape, BF16),
+                jax.ShapeDtypeStruct((rank, kt), F32),
+            ),
+            in_specs=[vmem] * 4,
+            out_specs=(hbm, vmem),
+            scratch_shapes=[pltpu.VMEM((width, kw), BF16), dma((width // tile,))],
+            compiler_params=pltpu.CompilerParams(vmem_limit_bytes=16 * mib),
+        )(merged, pcat, qcat, own_q)
+        return error_new, q.T
 
     return jax.shard_map(
         body,

time: 71.9 us -> 58.9 us (0.82); the launches traced: 71 us -> 58.7 us
  local copies, waits for them, and re-layouts: 10.3 us -> 0 us
  Pallas kernels: 60.1 us -> 58.1 us
    unnamed x2 -> x0, local copies, waits for them, and re-layouts: 7.32 us -> none
    pallas_call x1, Pallas kernels: 60.1 us -> 54.7 us  [body(): pl.pallas_call(functools.partial(kernel, (replicas, outer, inner, tens)),...]
    pallas_call x0 -> x1, Pallas kernels: none -> 3.37 us  [body(): pl.pallas_call(functools.partial(update_kernel, tile), out_shape=(jax.Sha...]
    pallas_call x1 -> x0, local copies, waits for them, and re-layouts: 1.69 us -> none  [body(): pl.pallas_call(functools.partial(kernel, (replicas, outer, inner, tens)),...]
    reshape x1 -> x0, local copies, waits for them, and re-layouts: 1.25 us -> none  [body(): pause_positions.reshape(1, -1)]
where the time goes in v2:
time: 58.9 us; the launch traced here: 58.7 us
  Pallas kernels  58.1 us (99%)
  between operations  0.64 us (1%)
    pallas_call x1, Pallas kernels, body(): pl.pallas_call(functools.partial(kernel, (replicas, outer, inner, tens)),...  54.7 us
    pallas_call x1, Pallas kernels, body(): pl.pallas_call(functools.partial(update_kernel, tile), out_shape=(jax.Sha...  3.37 us

profile of v2, /device:TPU:0, one launch (start us, length us, event | category | flops | bytes accessed | tf_op | source)
XLA Modules:
  0.0 58.7 jit_solution(16555786880879903658)
XLA Ops:
  0.6 54.7 %shard_map.68 = (f32[2560,1024]{1,0:T(8,128)S(1)}, bf16[96,2560]{1,0:T(8,128)(2,1)S(1)}, bf16[2,96,512]{2,1,0:T(8,128)(2,1)S(1)}, f32[32,512]{1,0:T(8,128)S(1)}) custom-call(bf16[1280,2560]{1,0:T(8,128)(2,1)} %act_hbm.1, bf16[1280,512]{1,0:T(8,128)(2,1)} %cot_hbm.1, bf16[2560,1024]{1,0:T(8,128)(2,1)} %err_hbm.1, s32[320]{0:T(512)} %pause_ref.1, ...), custom_call_target="tpu_custom_call" | custom-call | flops 6710886400 | bytes 17039360 | tf_op jit(solution)/shard_map/pallas_call | solution.py:330
  55.4 3.4 %shard_map.69 = (bf16[2560,1024]{1,0:T(8,128)(2,1)}, f32[32,512]{1,0:T(8,128)}) custom-call(f32[2560,1024]{1,0:T(8,128)S(1)} %get-tuple-element.8.merged, bf16[96,2560]{1,0:T(8,128)(2,1)S(1)} %get-tuple-element.9.pcat, bf16[2,96,512]{2,1,0:T(8,128)(2,1)S(1)} %get-tuple-element.10.qcat, f32[32,512]{1,0:T(8,128)S(1)} %get-tuple-element.11.q_in), custom_call_target="tpu_custom_call" | custom-call | tf_op jit(solution)/shard_map/pallas_call | solution.py:369

commit v3 on v2

--- a/solution.py
+++ b/solution.py
@@ -74,10 +74,10 @@
 def kernel(
     sizes, act_hbm, cot_hbm, err_hbm, pause_ref, q0_ref, merged, pcat, qcat, q_ref,
     act, cot, err, left_all, left3, parts, sum_in, qall,
-    xa1, ra1, xb1, rb1, gd1, xa2, ra2, xb2, rb2, gd2,
-    load_sem, t_send, t_recv, s1, r1, s2, r2,
+    xa1, ra1, xb1, rb1, gd1, xa2, ra2, xb2, rb2, gd2, xa3, ra3, xb3, rb3, gd3,
+    err_sem, act_sem, cot_sem, t_send, t_recv, s1, r1, s2, r2, s3, r3,
 ):
-    replicas, outer, inner, tens = sizes
+    replicas, outer, inner, tens, split, direct = sizes
     d = lax.axis_index("dp")
     t = lax.axis_index("tensor")
     o, i = d // inner, lax.rem(d, inner)
@@ -85,12 +85,22 @@
     kt = cot.shape[2]
     rank = q0_ref.shape[0]
 
-    load_err = pltpu.make_async_copy(err_hbm, err, load_sem.at[0])
-    load_cot = pltpu.make_async_copy(cot_hbm, cot.at[t], load_sem.at[1])
-    load_act = pltpu.make_async_copy(act_hbm, act, load_sem.at[2])
-    load_err.start()
+    loads = err_sem.shape[0]
+    load_cot = pltpu.make_async_copy(cot_hbm, cot.at[t], cot_sem.at[0])
     load_cot.start()
-    load_act.start()
+
+    def load(src, dst, sems):
+        step = src.shape[0] // loads
+        copies = []
+        for n in range(loads):
+            here = pl.ds(n * step, step)
+            copies.append(pltpu.make_async_copy(src.at[here], dst.at[here], sems.at[n]))
+        return copies
+
+    load_err = load(err_hbm, err, err_sem)
+    load_act = load(act_hbm, act, act_sem)
+    for copy in load_err:
+        copy.start()
 
     def outer_peer(k):
         return (lax.rem(o + k, outer) * inner + i, t)
@@ -98,12 +108,18 @@
     def inner_peer(k):
         return (o * inner + lax.rem(i + k, inner), t)
 
+    def any_peer(k):
+        return (lax.rem(d + k, replicas), t)
+
     def tensor_peer(k):
         return (d, lax.rem(t + k, tens))
 
     barrier = pltpu.get_barrier_semaphore()
-    peers = [outer_peer(k) for k in range(1, outer)]
-    peers += [inner_peer(k) for k in range(1, inner)]
+    if direct:
+        peers = [any_peer(k) for k in range(1, replicas)]
+    else:
+        peers = [outer_peer(k) for k in range(1, outer)]
+        peers += [inner_peer(k) for k in range(1, inner)]
     peers += [tensor_peer(k) for k in range(1, tens)]
     for peer in peers:
         pl.semaphore_signal(barrier, inc=1, device_id=peer, device_id_type=pl.DeviceIdType.MESH)
@@ -130,8 +146,13 @@
     kept = jnp.where(hits == 0.0, 1.0, 0.0).astype(BF16)
     q3 = stacked(q0_ref[...])
 
-    load_err.wait()
-    from_err = mm(q3, err[...], NT)
+    from_err = []
+    step = width // loads
+    for n, copy in enumerate(load_err):
+        copy.wait()
+        load_act[n].start()
+        from_err.append(mm(q3, err[n * step : (n + 1) * step], NT))
+    from_err = jnp.concatenate(from_err, axis=1)
     load_cot.wait()
     for copy in cot_copies:
         copy.wait_recv()
@@ -141,8 +162,12 @@
     for s in range(1, tens):
         tok = tok + mm(q3[:, s * kt : (s + 1) * kt], cot[s], NT)
     tok3 = stacked(folded(tok))
-    load_act.wait()
-    own_left = folded(mm(tok3, act[...], NN) + from_err) * (1.0 / replicas)
+    for copy in load_act:
+        copy.wait()
+
+    def left_part(first, last):
+        whole = mm(tok3, act[:, first:last], NN) + from_err[:, first:last]
+        return folded(whole) * (1.0 / replicas)
 
     tile = math.gcd(width, 256)
 
@@ -155,61 +180,72 @@
                 outs = slice(s * kt, (s + 1) * kt)
                 merged[here, outs] = mm(block, cot[s], TN) + err[here, outs].astype(F32)
 
-    def all_reduce(value, bufs, ss, rs, work):
+    def all_reduce(value, bufs, ss, rs, first, second):
+        (own1, n1, peer1), (own2, n2, peer2) = first, second
         xa, ra, xb, rb, gd = bufs
         h, span = xa.shape[1], value.shape[1]
         cw = xb.shape[2]
         if span < xa.shape[2]:
             xa[...] = jnp.zeros(xa.shape, F32)
-        for p in range(inner):
+        for p in range(n1):
             xa[p, :, :span] = value[p * h : (p + 1) * h]
         copies = [
-            send(xa.at[lax.rem(i + k, inner)], ra.at[k], ss.at[0, k], rs.at[0, k], inner_peer(k))
-            for k in range(1, inner)
+            send(xa.at[lax.rem(own1 + k, n1)], ra.at[k], ss.at[0, k], rs.at[0, k], peer1(k))
+            for k in range(1, n1)
         ]
-        work[0]()
-        total = xa[i]
+        yield
+        total = xa[own1]
         for k, copy in enumerate(copies, 1):
             copy.wait_recv()
             total = total + ra[k]
-        for p in range(outer):
-            xb[p] = total[:, p * cw : (p + 1) * cw]
+        if n2 > 1:
+            for p in range(n2):
+                xb[p] = total[:, p * cw : (p + 1) * cw]
+            copies = [
+                send(xb.at[lax.rem(own2 + k, n2)], rb.at[k], ss.at[1, k], rs.at[1, k], peer2(k))
+                for k in range(1, n2)
+            ]
+            yield
+            total = xb[own2]
+            for k, copy in enumerate(copies, 1):
+                copy.wait_recv()
+                total = total + rb[k]
+            gd[own1, own2] = total
+            copies = [
+                send(gd.at[own1, own2], gd.at[own1, own2], ss.at[2, k], rs.at[2, k], peer2(k))
+                for k in range(1, n2)
+            ]
+            yield
+            for copy in copies:
+                copy.wait_recv()
+        else:
+            gd[own1, 0] = total
         copies = [
-            send(xb.at[lax.rem(o + k, outer)], rb.at[k], ss.at[1, k], rs.at[1, k], outer_peer(k))
-            for k in range(1, outer)
+            send(gd.at[own1], gd.at[own1], ss.at[3, k], rs.at[3, k], peer1(k))
+            for k in range(1, n1)
         ]
-        work[1]()
-        total = xb[o]
-        for k, copy in enumerate(copies, 1):
-            copy.wait_recv()
-            total = total + rb[k]
-        gd[i, o] = total
-        copies = [
-            send(gd.at[i, o], gd.at[i, o], ss.at[2, k], rs.at[2, k], outer_peer(k))
-            for k in range(1, outer)
-        ]
-        work[2]()
-        for copy in copies:
-            copy.wait_recv()
-        copies = [
-            send(gd.at[i], gd.at[i], ss.at[3, k], rs.at[3, k], inner_peer(k))
-            for k in range(1, inner)
-        ]
-        work[3]()
+        yield
         for copy in copies:
             copy.wait_recv()
         bands = [
-            jnp.concatenate([gd[p, c] for c in range(outer)], axis=1)[:, :span]
-            for p in range(inner)
+            jnp.concatenate([gd[p, c] for c in range(n2)], axis=1)[:, :span]
+            for p in range(n1)
         ]
-        return jnp.concatenate(bands, axis=0)
-
+        yield jnp.concatenate(bands, axis=0)
+
+    by_inner = (i, inner, inner_peer)
+    by_outer = (o, outer, outer_peer)
     tiles = width // tile
-    marks = [tiles * n // 10 for n in (0, 3, 5, 7, 10)]
-    left = all_reduce(
-        own_left, (xa1, ra1, xb1, rb1, gd1), s1, r1,
-        [functools.partial(gradient_tiles, marks[n], marks[n + 1]) for n in range(4)],
-    )
+    marks = [tiles * n // 10 for n in (0, 3, 5, 7, 9)]
+    run1 = all_reduce(left_part(0, split), (xa1, ra1, xb1, rb1, gd1), s1, r1, by_outer, by_inner)
+    next(run1)
+    run2 = all_reduce(left_part(split, width), (xa2, ra2, xb2, rb2, gd2), s2, r2, by_inner, by_outer)
+    next(run2)
+    for n in range(4):
+        gradient_tiles(marks[n], marks[n + 1])
+        part2 = next(run2)
+        part1 = next(run1)
+    left = jnp.concatenate([part1, part2], axis=1)
     left_all[t] = left
     left_copies = [
         send(left_all.at[t], left_all.at[t], t_send.at[1, k], t_recv.at[1, k], tensor_peer(k))
@@ -254,17 +290,19 @@
         high, middle, _ = pieces(applied(held["inv2"], left3[t]))
         pcat[...] = jnp.concatenate([high, middle, high], axis=0)
 
-    def nothing():
-        pass
-
     second_gram()
     total = parts[t]
     for k, copy in enumerate(copies, 1):
         copy.wait_recv()
         total = total + sum_in[k]
-    total = all_reduce(
-        total, (xa2, ra2, xb2, rb2, gd2), s2, r2, [second_inverse, own_basis, nothing, nothing]
-    )
+    groups = ((d, replicas, any_peer), (0, 1, None)) if direct else (by_inner, by_outer)
+    run3 = all_reduce(total, (xa3, ra3, xb3, rb3, gd3), s3, r3, *groups)
+    next(run3)
+    second_inverse()
+    total = next(run3)
+    own_basis()
+    while total is None:
+        total = next(run3)
     own_q = mm_high(held["both"], total, NN)
     qall[t] = own_q
     copies = [
@@ -272,6 +310,7 @@
         for k in range(1, tens)
     ]
     q_ref[...] = own_q
+    gradient_tiles(marks[4], tiles)
     for copy in copies:
         copy.wait_recv()
     for s in range(tens):
@@ -310,25 +349,27 @@
         kt = cotangents.shape[1]
         kw, rank = initial_q.shape
         mib = 1024 * 1024
-        h = rank // inner
         tile = math.gcd(width, 256)
-
-        def reduce_bufs(span):
-            cw = -(-span // (128 * outer)) * 128
+        split = 2 * width // 5 // 128 * 128
+        direct = replicas <= min(rank, 16)
+        loads = 4 if width % 512 == 0 and rows % 64 == 0 else 1
+
+        def reduce_bufs(span, n1, n2):
+            h, cw = rank // n1, -(-span // (128 * n2)) * 128
             return [
-                pltpu.VMEM((inner, h, cw * outer), F32),
-                pltpu.VMEM((inner, h, cw * outer), F32),
-                pltpu.VMEM((outer, h, cw), F32),
-                pltpu.VMEM((outer, h, cw), F32),
-                pltpu.VMEM((inner, outer, h, cw), F32),
+                pltpu.VMEM((n1, h, cw * n2), F32),
+                pltpu.VMEM((n1, h, cw * n2), F32),
+                pltpu.VMEM((n2, h, cw), F32),
+                pltpu.VMEM((n2, h, cw), F32),
+                pltpu.VMEM((n1, n2, h, cw), F32),
             ]
 
-        most = max(inner, outer)
+        most = replicas if direct else max(inner, outer)
         hbm = pl.BlockSpec(memory_space=pltpu.HBM)
         vmem = pl.BlockSpec(memory_space=pltpu.VMEM)
         dma = pltpu.SemaphoreType.DMA
         merged, pcat, qcat, own_q = pl.pallas_call(
-            functools.partial(kernel, (replicas, outer, inner, tens)),
+            functools.partial(kernel, (replicas, outer, inner, tens, split, direct)),
             out_shape=(
                 pltpu.VMEM((width, kw), F32),
                 pltpu.VMEM((3 * rank, width), BF16),
@@ -346,15 +387,15 @@
                 pltpu.VMEM((tens, rank, kt), F32),
                 pltpu.VMEM((tens, rank, kt), F32),
                 pltpu.VMEM((tens, rank, kt), F32),
-                *reduce_bufs(width),
-                *reduce_bufs(kt),
-                dma((3,)),
+                *reduce_bufs(split, outer, inner),
+                *reduce_bufs(width - split, inner, outer),
+                *(reduce_bufs(kt, replicas, 1) if direct else reduce_bufs(kt, inner, outer)),
+                dma((loads,)),
+                dma((loads,)),
+                dma((1,)),
                 dma((4, tens)),
                 dma((4, tens)),
-                dma((4, most)),
-                dma((4, most)),
-                dma((4, most)),
-                dma((4, most)),
+                *[dma((4, most))] * 6,
             ],
             compiler_params=pltpu.CompilerParams(
                 collective_id=0, has_side_effects=True, vmem_limit_bytes=36 * mib

time: 58.9 us -> 57.4 us (0.975)
  Pallas kernels: 58.1 us -> 56.5 us
    pallas_call x1, Pallas kernels: 54.7 us -> 53.1 us  [body(): pl.pallas_call(functools.partial(kernel, (replicas, outer, inner, tens, s...]
where the time goes in v3:
time: 57.4 us; the launch traced here: 57.3 us
  Pallas kernels  56.5 us (98%)
  between operations  0.8 us (1%)
    pallas_call x1, Pallas kernels, body(): pl.pallas_call(functools.partial(kernel, (replicas, outer, inner, tens, s...  53.1 us
    pallas_call x1, Pallas kernels, body(): pl.pallas_call(functools.partial(update_kernel, tile), out_shape=(jax.Sha...  3.37 us

profile of v3, /device:TPU:0, one launch (start us, length us, event | category | flops | bytes accessed | tf_op | source)
XLA Modules:
  0.0 57.3 jit_solution(9054810677356552961)
XLA Ops:
  0.6 53.1 %shard_map.68 = (f32[2560,1024]{1,0:T(8,128)S(1)}, bf16[96,2560]{1,0:T(8,128)(2,1)S(1)}, bf16[2,96,512]{2,1,0:T(8,128)(2,1)S(1)}, f32[32,512]{1,0:T(8,128)S(1)}) custom-call(bf16[1280,2560]{1,0:T(8,128)(2,1)} %act_hbm.1, bf16[1280,512]{1,0:T(8,128)(2,1)} %cot_hbm.1, bf16[2560,1024]{1,0:T(8,128)(2,1)} %err_hbm.1, s32[320]{0:T(512)} %pause_ref.1, ...), custom_call_target="tpu_custom_call" | custom-call | flops 6710886400 | bytes 17039360 | tf_op jit(solution)/shard_map/pallas_call | solution.py:371
  53.7 3.4 %shard_map.69 = (bf16[2560,1024]{1,0:T(8,128)(2,1)}, f32[32,512]{1,0:T(8,128)}) custom-call(f32[2560,1024]{1,0:T(8,128)S(1)} %get-tuple-element.8.merged, bf16[96,2560]{1,0:T(8,128)(2,1)S(1)} %get-tuple-element.9.pcat, bf16[2,96,512]{2,1,0:T(8,128)(2,1)S(1)} %get-tuple-element.10.qcat, f32[32,512]{1,0:T(8,128)S(1)} %get-tuple-element.11.q_in), custom_call_target="tpu_custom_call" | custom-call | tf_op jit(solution)/shard_map/pallas_call | solution.py:410

commit v4 on v3

--- a/solution.py
+++ b/solution.py
@@ -12,7 +12,6 @@
 BF16 = jnp.bfloat16
 NN = (((1,), (0,)), ((), ()))
 NT = (((1,), (1,)), ((), ()))
-TN = (((0,), (0,)), ((), ()))
 
 
 def mm(a, b, dims):
@@ -59,11 +58,17 @@
     left = gram
     right = jnp.where(rows == cols, 1.0, 0.0).astype(F32)
     pivots = jnp.ones((n, n), F32)
+    group = math.gcd(n, 8)
     for k in range(n):
-        column = jnp.broadcast_to(left[:, k : k + 1], (n, n))
+        if k % group == 0:
+            spread = [jnp.broadcast_to(left[:, c : c + 1], (n, n)) for c in range(k, k + group)]
+        column = spread[k % group]
         pivots = jnp.where(rows == k, column, pivots)
         scale = 1.0 / column[k : k + 1, :]
         column = jnp.where(rows > k, column, 0.0)
+        for c in range(k % group + 1, group):
+            entry = column[k - k % group + c : k - k % group + c + 1, :] * scale
+            spread[c] = spread[c] - column * entry
         left_row = left[k : k + 1, :] * scale
         right_row = right[k : k + 1, :] * scale
         left = left - column * left_row
@@ -175,10 +180,10 @@
         @pl.loop(first, last)
         def _(j):
             here = pl.ds(pl.multiple_of(j * tile, tile), tile)
-            block = act[:, here]
+            block = act[:, here].T
             for s in range(tens):
                 outs = slice(s * kt, (s + 1) * kt)
-                merged[here, outs] = mm(block, cot[s], TN) + err[here, outs].astype(F32)
+                merged[here, outs] = mm(block, cot[s], NN) + err[here, outs].astype(F32)
 
     def all_reduce(value, bufs, ss, rs, first, second):
         (own1, n1, peer1), (own2, n2, peer2) = first, second
@@ -325,9 +330,10 @@
     copies = []
     for j in range(out.shape[0] // tile):
         here = slice(j * tile, (j + 1) * tile)
+        basis = pcat[:, here].T
         for s in range(tens):
             outs = slice(s * kt, (s + 1) * kt)
-            update = mm(pcat[:, here], qcat[s], TN)
+            update = mm(basis, qcat[s], NN)
             out[here, outs] = (merged[here, outs] - update).astype(BF16)
         copy = pltpu.make_async_copy(out.at[here], out_hbm.at[here], sems.at[j])
         copy.start()

time: 57.4 us -> 53.7 us (0.936)
  Pallas kernels: 56.5 us -> 52.8 us
    pallas_call x1, Pallas kernels: 53.1 us -> 49.4 us  [body(): pl.pallas_call(functools.partial(kernel, (replicas, outer, inner, tens, s...]
where the time goes in v4:
time: 53.7 us; the launch traced here: 53.6 us
  Pallas kernels  52.8 us (98%)
  between operations  0.8 us (1%)
    pallas_call x1, Pallas kernels, body(): pl.pallas_call(functools.partial(kernel, (replicas, outer, inner, tens, s...  49.4 us
    pallas_call x1, Pallas kernels, body(): pl.pallas_call(functools.partial(update_kernel, tile), out_shape=(jax.Sha...  3.37 us

profile of v4, /device:TPU:0, one launch (start us, length us, event | category | flops | bytes accessed | tf_op | source)
XLA Modules:
  0.0 53.6 jit_solution(15247287609758907778)
XLA Ops:
  0.6 49.4 %shard_map.68 = (f32[2560,1024]{1,0:T(8,128)S(1)}, bf16[96,2560]{1,0:T(8,128)(2,1)S(1)}, bf16[2,96,512]{2,1,0:T(8,128)(2,1)S(1)}, f32[32,512]{1,0:T(8,128)S(1)}) custom-call(bf16[1280,2560]{1,0:T(8,128)(2,1)} %act_hbm.1, bf16[1280,512]{1,0:T(8,128)(2,1)} %cot_hbm.1, bf16[2560,1024]{1,0:T(8,128)(2,1)} %err_hbm.1, s32[320]{0:T(512)} %pause_ref.1, ...), custom_call_target="tpu_custom_call" | custom-call | flops 6710886400 | bytes 17039360 | tf_op jit(solution)/shard_map/pallas_call | solution.py:377
  50.1 3.4 %shard_map.69 = (bf16[2560,1024]{1,0:T(8,128)(2,1)}, f32[32,512]{1,0:T(8,128)}) custom-call(f32[2560,1024]{1,0:T(8,128)S(1)} %get-tuple-element.8.merged, bf16[96,2560]{1,0:T(8,128)(2,1)S(1)} %get-tuple-element.9.pcat, bf16[2,96,512]{2,1,0:T(8,128)(2,1)S(1)} %get-tuple-element.10.qcat, f32[32,512]{1,0:T(8,128)S(1)} %get-tuple-element.11.q_in), custom_call_target="tpu_custom_call" | custom-call | tf_op jit(solution)/shard_map/pallas_call | solution.py:416

commit v5 on v4

--- a/solution.py
+++ b/solution.py
@@ -78,7 +78,7 @@
 
 def kernel(
     sizes, act_hbm, cot_hbm, err_hbm, pause_ref, q0_ref, merged, pcat, qcat, q_ref,
-    act, cot, err, left_all, left3, parts, sum_in, qall,
+    act, cot, err, q3, left_all, left3, parts, sum_in, qall,
     xa1, ra1, xb1, rb1, gd1, xa2, ra2, xb2, rb2, gd2, xa3, ra3, xb3, rb3, gd3,
     err_sem, act_sem, cot_sem, t_send, t_recv, s1, r1, s2, r2, s3, r3,
 ):
@@ -149,23 +149,26 @@
     positions = lax.broadcasted_iota(jnp.int32, (row_count, pause_ref.shape[0]), 0)
     hits = jnp.sum(jnp.where(positions == pause_ref[...].reshape(1, -1), 1.0, 0.0), axis=1, keepdims=True)
     kept = jnp.where(hits == 0.0, 1.0, 0.0).astype(BF16)
-    q3 = stacked(q0_ref[...])
+    q3[...] = stacked(q0_ref[...])
 
     from_err = []
     step = width // loads
     for n, copy in enumerate(load_err):
         copy.wait()
         load_act[n].start()
-        from_err.append(mm(q3, err[n * step : (n + 1) * step], NT))
+        from_err.append(mm(q3[...], err[n * step : (n + 1) * step], NT))
     from_err = jnp.concatenate(from_err, axis=1)
     load_cot.wait()
-    for copy in cot_copies:
+
+    def token_sums(s):
+        cot[s] = cot[s] * kept
+        outs = pl.ds(pl.multiple_of(s * kt, kt), kt)
+        return mm(q3[:, outs], cot[s], NT)
+
+    tok = token_sums(t)
+    for k, copy in enumerate(cot_copies, 1):
         copy.wait_recv()
-    for s in range(tens):
-        cot[s] = cot[s] * kept
-    tok = mm(q3[:, :kt], cot[0], NT)
-    for s in range(1, tens):
-        tok = tok + mm(q3[:, s * kt : (s + 1) * kt], cot[s], NT)
+        tok = tok + token_sums(lax.rem(t + tens - k, tens))
     tok3 = stacked(folded(tok))
     for copy in load_act:
         copy.wait()
@@ -174,12 +177,12 @@
         whole = mm(tok3, act[:, first:last], NN) + from_err[:, first:last]
         return folded(whole) * (1.0 / replicas)
 
-    tile = math.gcd(width, 256)
+    tile = width // 5 if width % 640 == 0 else math.gcd(width, 256)
+    tiles = width // tile
 
     def gradient_tiles(first, last):
-        @pl.loop(first, last)
-        def _(j):
-            here = pl.ds(pl.multiple_of(j * tile, tile), tile)
+        for j in range(first, last):
+            here = slice(j * tile, (j + 1) * tile)
             block = act[:, here].T
             for s in range(tens):
                 outs = slice(s * kt, (s + 1) * kt)
@@ -240,8 +243,7 @@
 
     by_inner = (i, inner, inner_peer)
     by_outer = (o, outer, outer_peer)
-    tiles = width // tile
-    marks = [tiles * n // 10 for n in (0, 3, 5, 7, 9)]
+    marks = [tiles * n // 5 for n in range(5)]
     run1 = all_reduce(left_part(0, split), (xa1, ra1, xb1, rb1, gd1), s1, r1, by_outer, by_inner)
     next(run1)
     run2 = all_reduce(left_part(split, width), (xa2, ra2, xb2, rb2, gd2), s2, r2, by_inner, by_outer)
@@ -388,6 +390,7 @@
                 pltpu.VMEM((rows, width), BF16),
                 pltpu.VMEM((tens, rows, kt), BF16),
                 pltpu.VMEM((width, kw), BF16),
+                pltpu.VMEM((3 * rank, kw), BF16),
                 pltpu.VMEM((tens, rank, width), F32),
                 pltpu.VMEM((tens, 3 * rank, width), BF16),
                 pltpu.VMEM((tens, rank, kt), F32),

time: 53.7 us -> 54.6 us (1.017)
  Pallas kernels: 52.8 us -> 53.6 us
    pallas_call x1, Pallas kernels: 49.4 us -> 50.3 us  [body(): pl.pallas_call(functools.partial(kernel, (replicas, outer, inner, tens, s...]
where the time goes in v5:
time: 54.6 us; the launch traced here: 54.4 us
  Pallas kernels  53.6 us (98%)
  between operations  0.8 us (1%)
    pallas_call x1, Pallas kernels, body(): pl.pallas_call(functools.partial(kernel, (replicas, outer, inner, tens, s...  50.3 us
    pallas_call x1, Pallas kernels, body(): pl.pallas_call(functools.partial(update_kernel, tile), out_shape=(jax.Sha...  3.36 us

profile of v5, /device:TPU:0, one launch (start us, length us, event | category | flops | bytes accessed | tf_op | source)
XLA Modules:
  0.0 54.4 jit_solution(8142020163859610516)
XLA Ops:
  0.6 50.3 %shard_map.68 = (f32[2560,1024]{1,0:T(8,128)S(1)}, bf16[96,2560]{1,0:T(8,128)(2,1)S(1)}, bf16[2,96,512]{2,1,0:T(8,128)(2,1)S(1)}, f32[32,512]{1,0:T(8,128)S(1)}) custom-call(bf16[1280,2560]{1,0:T(8,128)(2,1)} %act_hbm.1, bf16[1280,512]{1,0:T(8,128)(2,1)} %cot_hbm.1, bf16[2560,1024]{1,0:T(8,128)(2,1)} %err_hbm.1, s32[320]{0:T(512)} %pause_ref.1, ...), custom_call_target="tpu_custom_call" | custom-call | flops 6710886400 | bytes 17039360 | tf_op jit(solution)/shard_map/pallas_call | solution.py:379
  50.9 3.4 %shard_map.69 = (bf16[2560,1024]{1,0:T(8,128)(2,1)}, f32[32,512]{1,0:T(8,128)}) custom-call(f32[2560,1024]{1,0:T(8,128)S(1)} %get-tuple-element.8.merged, bf16[96,2560]{1,0:T(8,128)(2,1)S(1)} %get-tuple-element.9.pcat, bf16[2,96,512]{2,1,0:T(8,128)(2,1)S(1)} %get-tuple-element.10.qcat, f32[32,512]{1,0:T(8,128)S(1)} %get-tuple-element.11.q_in), custom_call_target="tpu_custom_call" | custom-call | tf_op jit(solution)/shard_map/pallas_call | solution.py:419

commit v6 on v5

--- a/solution.py
+++ b/solution.py
@@ -78,7 +78,7 @@
 
 def kernel(
     sizes, act_hbm, cot_hbm, err_hbm, pause_ref, q0_ref, merged, pcat, qcat, q_ref,
-    act, cot, err, q3, left_all, left3, parts, sum_in, qall,
+    act, cot, err, q3, turned, left_all, left3, parts, sum_in, qall,
     xa1, ra1, xb1, rb1, gd1, xa2, ra2, xb2, rb2, gd2, xa3, ra3, xb3, rb3, gd3,
     err_sem, act_sem, cot_sem, t_send, t_recv, s1, r1, s2, r2, s3, r3,
 ):
@@ -151,6 +151,13 @@
     kept = jnp.where(hits == 0.0, 1.0, 0.0).astype(BF16)
     q3[...] = stacked(q0_ref[...])
 
+    def token_sums(s):
+        cot[s] = cot[s] * kept
+        outs = pl.ds(pl.multiple_of(s * kt, kt), kt)
+        return mm(q3[:, outs], cot[s], NT)
+
+    load_cot.wait()
+    tok = token_sums(t)
     from_err = []
     step = width // loads
     for n, copy in enumerate(load_err):
@@ -158,14 +165,6 @@
         load_act[n].start()
         from_err.append(mm(q3[...], err[n * step : (n + 1) * step], NT))
     from_err = jnp.concatenate(from_err, axis=1)
-    load_cot.wait()
-
-    def token_sums(s):
-        cot[s] = cot[s] * kept
-        outs = pl.ds(pl.multiple_of(s * kt, kt), kt)
-        return mm(q3[:, outs], cot[s], NT)
-
-    tok = token_sums(t)
     for k, copy in enumerate(cot_copies, 1):
         copy.wait_recv()
         tok = tok + token_sums(lax.rem(t + tens - k, tens))
@@ -177,13 +176,15 @@
         whole = mm(tok3, act[:, first:last], NN) + from_err[:, first:last]
         return folded(whole) * (1.0 / replicas)
 
-    tile = width // 5 if width % 640 == 0 else math.gcd(width, 256)
+    tile = math.gcd(width, 256)
     tiles = width // tile
 
     def gradient_tiles(first, last):
-        for j in range(first, last):
-            here = slice(j * tile, (j + 1) * tile)
+        @pl.loop(first, last)
+        def _(j):
+            here = pl.ds(pl.multiple_of(j * tile, tile), tile)
             block = act[:, here].T
+            turned[here] = block
             for s in range(tens):
                 outs = slice(s * kt, (s + 1) * kt)
                 merged[here, outs] = mm(block, cot[s], NN) + err[here, outs].astype(F32)
@@ -243,7 +244,7 @@
 
     by_inner = (i, inner, inner_peer)
     by_outer = (o, outer, outer_peer)
-    marks = [tiles * n // 5 for n in range(5)]
+    marks = [tiles * n // 10 for n in (0, 3, 5, 7, 10)]
     run1 = all_reduce(left_part(0, split), (xa1, ra1, xb1, rb1, gd1), s1, r1, by_outer, by_inner)
     next(run1)
     run2 = all_reduce(left_part(split, width), (xa2, ra2, xb2, rb2, gd2), s2, r2, by_inner, by_outer)
@@ -261,7 +262,7 @@
 
     own3 = stacked(left)
     left3[t] = own3
-    v3 = stacked(folded(mm(own3, act[...], NT)))
+    v3 = stacked(folded(mm(own3, turned[...], NN)))
     for copy in left_copies:
         copy.wait_recv()
     for k in range(1, tens):
@@ -317,7 +318,6 @@
         for k in range(1, tens)
     ]
     q_ref[...] = own_q
-    gradient_tiles(marks[4], tiles)
     for copy in copies:
         copy.wait_recv()
     for s in range(tens):
@@ -391,6 +391,7 @@
                 pltpu.VMEM((tens, rows, kt), BF16),
                 pltpu.VMEM((width, kw), BF16),
                 pltpu.VMEM((3 * rank, kw), BF16),
+                pltpu.VMEM((width, rows), BF16),
                 pltpu.VMEM((tens, rank, width), F32),
                 pltpu.VMEM((tens, 3 * rank, width), BF16),
                 pltpu.VMEM((tens, rank, kt), F32),

time: 54.6 us -> 52.6 us (0.963)
  Pallas kernels: 53.6 us -> 51.6 us
    pallas_call x1, Pallas kernels: 50.3 us -> 48.3 us  [body(): pl.pallas_call(functools.partial(kernel, (replicas, outer, inner, tens, s...]
where the time goes in v6:
time: 52.6 us; the launch traced here: 52.4 us
  Pallas kernels  51.6 us (98%)
  between operations  0.8 us (2%)
    pallas_call x1, Pallas kernels, body(): pl.pallas_call(functools.partial(kernel, (replicas, outer, inner, tens, s...  48.3 us
    pallas_call x1, Pallas kernels, body(): pl.pallas_call(functools.partial(update_kernel, tile), out_shape=(jax.Sha...  3.37 us

profile of v6, /device:TPU:0, one launch (start us, length us, event | category | flops | bytes accessed | tf_op | source)
XLA Modules:
  0.0 52.4 jit_solution(16877126537493315844)
XLA Ops:
  0.6 48.3 %shard_map.68 = (f32[2560,1024]{1,0:T(8,128)S(1)}, bf16[96,2560]{1,0:T(8,128)(2,1)S(1)}, bf16[2,96,512]{2,1,0:T(8,128)(2,1)S(1)}, f32[32,512]{1,0:T(8,128)S(1)}) custom-call(bf16[1280,2560]{1,0:T(8,128)(2,1)} %act_hbm.1, bf16[1280,512]{1,0:T(8,128)(2,1)} %cot_hbm.1, bf16[2560,1024]{1,0:T(8,128)(2,1)} %err_hbm.1, s32[320]{0:T(512)} %pause_ref.1, ...), custom_call_target="tpu_custom_call" | custom-call | flops 6710886400 | bytes 17039360 | tf_op jit(solution)/shard_map/pallas_call | solution.py:379
  48.9 3.4 %shard_map.69 = (bf16[2560,1024]{1,0:T(8,128)(2,1)}, f32[32,512]{1,0:T(8,128)}) custom-call(f32[2560,1024]{1,0:T(8,128)S(1)} %get-tuple-element.8.merged, bf16[96,2560]{1,0:T(8,128)(2,1)S(1)} %get-tuple-element.9.pcat, bf16[2,96,512]{2,1,0:T(8,128)(2,1)S(1)} %get-tuple-element.10.qcat, f32[32,512]{1,0:T(8,128)S(1)} %get-tuple-element.11.q_in), custom_call_target="tpu_custom_call" | custom-call | tf_op jit(solution)/shard_map/pallas_call | solution.py:420
